TPU v7x, 512 devices: a whole 4x8x8 slice. The times are simulated.
512 devices in a mesh: row: 64 (over x, z, core), col: 8 (over y).
Axes of the slice: x: 4, y: 8, z: 8, core: 2. Of those that a mesh axis runs over, the one named last changes fastest.
Arguments:
- image: float32 [16384, 768], P(('row', 'col')), may hold values from -4 to 4
- text: float32 [16384, 768], P(('col', 'row')), may hold values from -4 to 4
Outputs:
- loss: float32 [], replicated
- image_grad: float32 [16384, 768], P(('row', 'col'))
- text_grad: float32 [16384, 768], P(('col', 'row'))
All inputs are finite; a program needn't handle non-finite values.
Results may differ from a plain program's by a relative error of at most 0.0003.
Values sent between devices are 32-bit elements; how exact they have to be, the bound alone decides.
A program may use at most 64 MiB of HBM per device.

v0:
```python
import jax
import jax.numpy as jnp
from jax import lax
from jax.sharding import PartitionSpec as P

logit_scale = 20.0


def local(image, text):
    row_count = lax.axis_size("row")
    col_count = lax.axis_size("col")
    shard_rows = image.shape[0]
    row_pos = lax.axis_index("row")
    col_pos = lax.axis_index("col")
    img_rows = lax.all_gather(image, "col", axis=0, tiled=True)
    slab_rows = img_rows.shape[0]
    txt_tile = lax.all_gather(text, "row", axis=0, tiled=True)
    row_first = row_pos * slab_rows
    col_ids = col_pos * txt_tile.shape[0] + jnp.arange(txt_tile.shape[0])
    own_row = col_pos * shard_rows
    own_col = row_pos * shard_rows
    logits = logit_scale * lax.dot_general(
        img_rows,
        txt_tile,
        (((1,), (1,)), ((), ())),
        precision=lax.Precision.HIGHEST,
        preferred_element_type=jnp.float32,
    )
    peak_here = jnp.max(logits, axis=1)
    colpeak_here = jnp.max(logits, axis=0)
    row_peak = lax.pmax(peak_here, "col")
    row_total = lax.psum(jnp.sum(jnp.exp(logits - row_peak[:, None]), axis=1), "col")
    col_peak = lax.pmax(colpeak_here, "row")
    coltotal_here = jnp.sum(jnp.exp(logits - col_peak[None, :]), axis=0)
    col_total = lax.psum(coltotal_here, "row")
    row_lse = row_peak + jnp.log(row_total)
    col_lse = col_peak + jnp.log(col_total)
    row_ids = row_first + jnp.arange(img_rows.shape[0])
    is_diag = row_ids[:, None] == col_ids[None, :]
    own_rows = lax.dynamic_slice_in_dim(row_lse, own_row, shard_rows)
    own_cols = lax.dynamic_slice_in_dim(col_lse, own_col, shard_rows)
    partial_loss = (
        jnp.sum(own_rows) + jnp.sum(own_cols) - 2.0 * jnp.sum(jnp.where(is_diag, logits, 0.0))
    )
    batch_total = shard_rows * row_count * col_count
    loss = lax.psum(partial_loss, ("row", "col")) / (2.0 * batch_total)
    weights = (
        jnp.exp(logits - row_lse[:, None])
        + jnp.exp(logits - col_lse[None, :])
        - 2.0 * is_diag.astype(jnp.float32)
    )
    image_terms = (
        0.5
        * logit_scale
        * jnp.dot(
            weights, txt_tile, precision=lax.Precision.HIGHEST, preferred_element_type=jnp.float32
        )
    )
    text_terms = (
        0.5
        * logit_scale
        * lax.dot_general(
            weights,
            img_rows,
            (((0,), (0,)), ((), ())),
            precision=lax.Precision.HIGHEST,
            preferred_element_type=jnp.float32,
        )
    )
    text_grad = lax.psum_scatter(text_terms, "row", scatter_dimension=0, tiled=True)
    image_grad = lax.psum_scatter(image_terms, "col", scatter_dimension=0, tiled=True)
    return (loss, image_grad, text_grad)


def solution(mesh):
    in_specs = (P(("row", "col"), None), P(("col", "row"), None))
    out_specs = (P(), P(("row", "col"), None), P(("col", "row"), None))
    return jax.shard_map(local, mesh=mesh, in_specs=in_specs, out_specs=out_specs, check_vma=False)
```

profile of v0, /device:TPU:1, one launch (start us, length us, event | category | flops | bytes accessed | tf_op | source)
XLA Modules:
  0.0 605.7 jit_solution(14838921884735056350)
XLA Ops:
  7.2 0.0 all-gather.2.cloned.1.call-start
  7.2 0.7 all-gather.2.cloned.1.call-update
  7.9 0.0 reduce-scatter.3.cloned.1.call-start
  8.0 23.0 %all_gather.6 = f32[256,768]{1,0:T(8,128)S(1)} all-gather(f32[32,768]{1,0:T(8,128)} %param.2), channel_id=1, replica_groups=mesh['row'=64,'col'=8] {'col'}, dimensions={0}, use_global_device_ids=true | all-gather | bytes 884736 | tf_op jit(solution)/shard_map/all_gather | solution.py:15
  31.0 73.3 %all-gather.2.cloned.1.call-done = f32[2048,768]{1,0:T(8,128)} async-done(((f32[32,768]{1,0:T(8,128)}), f32[2048,768]{1,0:T(8,128)}) %all-gather.2.cloned.1.call-update) | async-done | bytes 6291472 | tf_op jit(solution)/shard_map/all_gather | solution.py:17
  104.3 7.7 %fusion.20 = (f32[2048]{0:T(1024)S(1)}, f32[256]{0:T(256)S(1)}, f32[256,2048]{1,0:T(8,128)S(1)}) fusion(f32[256,768]{1,0:T(8,128)S(1)} %all_gather.6, f32[2048,768]{1,0:T(8,128)} %all-gather.2.cloned.1.call-done), kind=kOutput, calls=%fused_computation.31 | convolution fusion | flops 4833409024 | bytes 9184256 | tf_op jit(solution)/shard_map/dot_general | solution.py:22
  112.1 125.7 %pmax.15 = f32[2048]{0:T(1024)S(1)} all-reduce(f32[2048]{0:T(1024)S(1)} %get-tuple-element.6), channel_id=1, replica_groups=mesh['row'=64,'col'=8] {'row'}, use_global_device_ids=true, to_apply=%region_6.0 | all-reduce | flops 2048 | bytes 16384 | tf_op jit(solution)/shard_map/pmax | solution.py:33
  237.7 13.2 %pmax.14 = f32[256]{0:T(256)S(1)} all-reduce(f32[256]{0:T(256)S(1)} %get-tuple-element.7), channel_id=1, replica_groups=mesh['row'=64,'col'=8] {'col'}, use_global_device_ids=true, to_apply=%region_1.0 | all-reduce | flops 256 | bytes 2048 | tf_op jit(solution)/shard_map/pmax | solution.py:31
  251.0 1.8 fusion
  252.8 131.9 %psum.22 = f32[2048]{0:T(1024)S(1)} all-reduce(f32[2048]{0:T(1024)S(1)} %get-tuple-element.4), channel_id=1, replica_groups=mesh['row'=64,'col'=8] {'row'}, use_global_device_ids=true, to_apply=%region_8.0 | all-reduce | flops 2048 | bytes 16384 | tf_op jit(solution)/shard_map/psum | solution.py:35
  384.7 11.5 %psum.21 = f32[256]{0:T(256)S(1)} all-reduce(f32[256]{0:T(256)S(1)} %get-tuple-element.5), channel_id=1, replica_groups=mesh['row'=64,'col'=8] {'col'}, use_global_device_ids=true, to_apply=%region_3.0 | all-reduce | flops 256 | bytes 2048 | tf_op jit(solution)/shard_map/psum | solution.py:32
  396.2 9.7 %convolution_multiply_fusion.2 = f32[256,768]{1,0:T(8,128)} fusion(f32[2048,768]{1,0:T(8,128)} %all-gather.2.cloned.1.call-done, f32[256,2048]{1,0:T(8,128)S(1)} %get-tuple-element.8, f32[2048]{0:T(1024)S(1)} %log_add_fusion, f32[256]{0:T(256)S(1)} %log_add_fusion.1, s32[2048]{0:T(1024)S(1)} %iota_add_fusion, s32[256]{0:T(256)S(1)} %iota_add_fusion.1), kind=kOutput, calls=%fused_computation.8 | convolution fusion | flops 4835180544 | bytes 9193472 | tf_op jit(solution)/shard_map/dot_general | solution.py:55
  405.8 0.0 reduce-scatter.3.cloned.1.call-update
  405.9 0.2 reduce-scatter.5.cloned.1.call-start
  406.1 7.8 %convolution_multiply_fusion = f32[2048,768]{1,0:T(8,128)} fusion(f32[256,768]{1,0:T(8,128)S(1)} %all_gather.6, f32[256,2048]{1,0:T(8,128)S(1)} %get-tuple-element.8, f32[2048]{0:T(1024)S(1)} %log_add_fusion, f32[256]{0:T(256)S(1)} %log_add_fusion.1, s32[2048]{0:T(1024)S(1)} %iota_add_fusion, s32[256]{0:T(256)S(1)} %iota_add_fusion.1), kind=kOutput, calls=%fused_computation | convolution fusion | flops 4836556800 | bytes 9193472 | tf_op jit(solution)/shard_map/dot_general | solution.py:62
  413.9 0.0 reduce-scatter.5.cloned.1.call-update
  413.9 0.7 dynamic-slice_reduce_fusion
  414.6 0.7 dynamic-slice_reduce_fusion.1
  417.2 97.2 %psum.23 = f32[]{:T(128)} all-reduce(f32[]{:T(128)S(6)} %sub.42), channel_id=1, replica_groups=mesh['row'=64,'col'=8] {'row','col'}, use_global_device_ids=true, to_apply=%region_11.12 | all-reduce | flops 1 | bytes 8 | tf_op jit(solution)/shard_map/psum | solution.py:46
  515.1 0.0 reduce-scatter.3.cloned.1.call-done
  515.1 83.0 %reduce-scatter.5.cloned.1.call-done = f32[32,768]{1,0:T(8,128)} async-done(((f32[2048,768]{1,0:T(8,128)}), f32[32,768]{1,0:T(8,128)}) %reduce-scatter.5.cloned.1.call-update) | async-done | bytes 98320 | tf_op jit(solution)/shard_map/reduce_scatter | solution.py:70
  (4 shorter events, 0.0 us)
Async XLA Ops:
  7.2 97.2 %all-gather.2.cloned.1.call-start = ((), (), s32[]{:S(2)}) async-start(), calls=%async_computation.2 | async-start | bytes 6389760 | tf_op jit(solution)/shard_map/all_gather | solution.py:17
  7.9 507.2 %reduce-scatter.3.cloned.1.call-start = ((), (), s32[]{:S(2)}) async-start(), calls=%async_computation.3 | async-start | bytes 884736 | tf_op jit(solution)/shard_map/reduce_scatter | solution.py:71
  405.9 192.2 %reduce-scatter.5.cloned.1.call-start = ((), (), s32[]{:S(2)}) async-start(), calls=%async_computation.4 | async-start | bytes 6389760 | tf_op jit(solution)/shard_map/reduce_scatter | solution.py:70
Sparse Core Ops, SparseCore 0:
  11.3 92.9 all-gather.1
  406.0 30.7 reduce-scatter.2
  442.8 155.2 reduce-scatter.4
where the time goes:
time: 610 us; the launch traced here: 606 us
  blocking collectives  402 us (66%)
  waiting for transfers between devices  157 us (26%)
  matrix products  25.2 us (4%)
  between operations  17.5 us (3%)
    psum x1, blocking collectives, local(): col_total = lax.psum(coltotal_here, 'row')  132 us
    pmax x1, blocking collectives, local(): col_peak = lax.pmax(colpeak_here, 'row')  126 us
    psum x1, blocking collectives, local(): loss = lax.psum(partial_loss, ('row', 'col')) / (2.0 * batch_total)  97.2 us
    reduce_scatter x1, waiting for transfers between devices, local(): lax.psum_scatter(text_terms, 'row', scatter_dimension=0, tiled=True)  83 us
    all_gather x1, waiting for transfers between devices, local(): txt_tile = lax.all_gather(text, 'row', axis=0, tiled=True)  73.3 us
    all_gather x1, blocking collectives, local(): img_rows = lax.all_gather(image, 'col', axis=0, tiled=True)  23 us
    pmax x1, blocking collectives, local(): row_peak = lax.pmax(peak_here, 'col')  13.2 us
  transfers between devices with their start and end apart: 3, of which 2 were waited for; matrix products, arithmetic and copies ran while one was open for 2% of the time, Pallas kernels for 0%

commit v1 on v0

v1 whole, which is shorter than its diff:
```python
import functools
import jax
import jax.numpy as jnp
from jax import lax
from jax.experimental import pallas as pl
from jax.experimental.pallas import tpu as pltpu
from jax.sharding import PartitionSpec as P

logit_scale = 20.0
grad_scale = 0.5 * logit_scale
MESH = pl.DeviceIdType.MESH
XN = 4
CORES = 2
H = 16
G = 4 * H
f32 = jnp.float32
bf16 = jnp.bfloat16
NT = (((1,), (1,)), ((), ()))
NN = (((1,), (0,)), ((), ()))
TN = (((0,), (0,)), ((), ()))


def dot3(a_hi, a_lo, b_hi, b_lo, dims):
    def dot(a, b):
        return lax.dot_general(a, b, dims, preferred_element_type=f32)

    return dot(a_hi, b_hi) + (dot(a_hi, b_lo) + dot(a_lo, b_hi))


def split(value):
    high = value.astype(bf16)
    return high, (value - high.astype(f32)).astype(bf16)


def merge(parts):
    peak = functools.reduce(jnp.maximum, [p for p, _ in parts])
    total = functools.reduce(jnp.add, [t * jnp.exp(p - peak) for p, t in parts])
    return peak, total


class Comm:
    def __init__(self, send_sem, recv_sem):
        self.send_sem, self.recv_sem, self.copies = send_sem, recv_sem, []

    def send(self, src, dst, device):
        i = len(self.copies)
        copy = pltpu.make_async_remote_copy(
            src_ref=src,
            dst_ref=dst,
            send_sem=self.send_sem.at[i],
            recv_sem=self.recv_sem.at[i],
            device_id=device,
            device_id_type=MESH,
        )
        copy.start()
        self.copies.append(copy)
        return copy

    def drain(self):
        for copy in self.copies:
            copy.wait_send()


class Gather:
    def __init__(self, comm, buf, own, n, up, down, partner, other):
        self.comm, self.buf, self.n = comm, buf, n
        self.up, self.down, self.partner, self.other = up, down, partner, other
        self.ahead, self.behind = n // 2, n - 1 - n // 2
        buf[0, 0:H] = own[0:H]
        buf[0, 2 * H : 3 * H] = own[H : 2 * H]
        self.cross, self.ring_p, self.ring_q, self.core = {}, {}, {}, {}
        self.q_cross = self._copy(buf.at[0, 2 * H : 3 * H], buf.at[0, 3 * H : 4 * H], partner)
        self._forward(0, 0, self.ring_p, 0, 2 * H // 2)
        self._forward_back(0, self.ring_p, 0, H)
        self._cross(0)

    def _copy(self, src, dst, device):
        return self.comm.send(src, dst, device)

    def _forward(self, k, _, ring, lo, hi):
        if k < self.ahead:
            ring[k + 1] = self._copy(self.buf.at[k, lo:hi], self.buf.at[k + 1, lo:hi], self.down)

    def _forward_back(self, k, ring, lo, hi):
        if k < self.behind:
            src, dst = (self.n - k) % self.n, self.n - k - 1
            ring[dst] = self._copy(self.buf.at[src, lo:hi], self.buf.at[dst, lo:hi], self.up)

    def _cross(self, k):
        self.cross[k] = self._copy(self.buf.at[k, 0:H], self.buf.at[k, H : 2 * H], self.partner)

    def start_q(self):
        self.q_cross.wait_recv()
        self._forward(0, 0, self.ring_q, 2 * H, G)
        self._forward_back(0, self.ring_q, 2 * H, G)

    def positions(self, s):
        if s == 0:
            return [0]
        return [s] + ([self.n - s] if s <= self.behind else [])

    def step_p(self, s):
        for k in self.positions(s):
            self.ring_p[k].wait_recv()
            if k == s:
                self._forward(k, 0, self.ring_p, 0, H)
            else:
                self._forward_back(s, self.ring_p, 0, H)
            self._cross(k)

    def step_q(self, s):
        for k in self.positions(s):
            self.ring_q[k].wait_recv()
            if k == s:
                self._forward(k, 0, self.ring_q, 2 * H, G)
            else:
                self._forward_back(s, self.ring_q, 2 * H, G)

    def finish(self, s):
        for k in self.positions(s):
            self.cross[k].wait_recv()
            if self.other is not None:
                to = (self.n - k) % self.n
                self.core[to] = self._copy(self.buf.at[k, 0:G], self.buf.at[to, G : 2 * G], self.other)


class Scatter:
    def __init__(self, comm, acc, cross_buf, p_up, p_down, q_up, q_down, q_cross, n, up, down, partner):
        self.comm, self.acc, self.cross_buf, self.n = comm, acc, cross_buf, n
        self.bufs = {"p": (p_up, p_down), "q": (q_up, q_down)}
        self.q_cross_buf = q_cross
        self.up, self.down, self.partner = up, down, partner
        self.ahead, self.behind = n // 2, n - 1 - n // 2
        self.cross, self.rings = {}, {}

    def rows(self, half):
        return slice(0, H) if half == "p" else slice(2 * H, G)

    def send_cross(self, k):
        self.cross[k] = self.comm.send(self.acc.at[k, H : 2 * H], self.cross_buf.at[k], self.partner)

    def add_cross(self, k):
        self.cross[k].wait_recv()
        self.acc[k, 0:H] += self.cross_buf[k]

    def launch(self, half, k):
        rows = self.rows(half)
        if k <= self.ahead:
            buf, step, device, key = self.bufs[half][0], self.ahead - k, self.up, (half, k - 1)
        else:
            back = self.n - k
            buf, step, device = self.bufs[half][1], self.behind - back, self.down
            key = (half, (k + 1) % self.n, "back")
        self.rings[key] = (self.comm.send(self.acc.at[k, rows], buf.at[step], device), buf, step)

    def take(self, half, k, back=False):
        key = (half, k, "back") if back else (half, k)
        copy, buf, step = self.rings[key]
        copy.wait_recv()
        self.acc[k, self.rows(half)] += buf[step]

    def step(self, half, s):
        k = self.ahead - s
        if k >= 0:
            self.take(half, k)
            if k > 0:
                self.launch(half, k)
        back = self.behind - s
        if back >= 0 and self.behind > 0:
            k = (self.n - back) % self.n
            self.take(half, k, True)
            if k:
                self.launch(half, k)

    def finish_q(self):
        self.last = self.comm.send(self.acc.at[0, 3 * H : 4 * H], self.q_cross_buf, self.partner)

    def result(self, out):
        out[0:H] = self.acc[0, 0:H] * grad_scale
        self.last.wait_recv()
        out[H : 2 * H] = (self.acc[0, 2 * H : 3 * H] + self.q_cross_buf[...]) * grad_scale


def kernel(nz, ny, image, text, loss, image_grad, text_grad,
           T, I, Th, Tl, Ih, Il, L, Er, Wh, Wl, TP, CR, IP,
           tx, tpu_, tpd, tqu, tqd, tqx, ix, ipu, ipd, iqu, iqd, iqx,
           St, Si, R1t, R1i, R2t, R2i, Ft, Fi, L1, L2, L3, send_sem, recv_sem):
    row, y = lax.axis_index("row"), lax.axis_index("col")
    x, z, c = row // (CORES * nz), (row // CORES) % nz, row % CORES
    turn = 1 - 2 * c
    xt = x + 1 - 2 * (x % 2)
    xi = XN - 1 - x

    def at(x_=x, y_=y, z_=z, c_=c):
        return (x_ * (CORES * nz) + z_ * CORES + c_, y_)

    def ring_z(k):
        return at(z_=(z + turn * k + nz) % nz)

    def ring_y(k):
        return at(y_=(y + turn * k + ny) % ny)

    def plane(i):
        j = (x * CORES + c + i) % (XN * CORES)
        return at(x_=j // CORES, c_=j % CORES)

    other = at(c_=1 - c)
    cols, rws = nz * 2 * G, ny * G
    comm = Comm(send_sem, recv_sem)

    barrier = pltpu.get_barrier_semaphore()
    peers = [ring_z(k) for k in range(1, nz)] + [ring_y(k) for k in range(1, ny)]
    peers += [plane(i) for i in range(1, XN * CORES)]
    for peer in peers:
        pl.semaphore_signal(barrier, inc=1, device_id=peer, device_id_type=MESH)
    pl.semaphore_wait(barrier, len(peers))

    gt = Gather(comm, T, text, nz, ring_z(1), ring_z(nz - 1), at(x_=xt), other)
    gi = Gather(comm, I, image, ny, ring_y(1), ring_y(ny - 1), at(x_=xi), None)
    gt.start_q()
    gi.start_q()
    steps = max(nz, ny) // 2 + 1
    for s in range(steps):
        for g in (gt, gi):
            if 1 <= s <= g.ahead:
                g.step_p(s)
        for g in (gt, gi):
            if 1 <= s <= g.ahead:
                g.step_q(s)
        for g in (gt, gi):
            if s <= g.ahead:
                g.finish(s)
    for k in range(ny):
        Ih[k * G : (k + 1) * G], Il[k * G : (k + 1) * G] = split(I[k])
    for k in range(nz):
        gt.core[k].wait_recv()
        first = k * 2 * G
        Th[first : first + 2 * G], Tl[first : first + 2 * G] = split(T[k])

    block = min(256, cols)
    blocks = cols // block
    for b in range(blocks):
        span = slice(b * block, (b + 1) * block)
        L[:, span] = logit_scale * dot3(Ih[...], Il[...], Th[span], Tl[span], NT)

    def iota(shape, dim):
        return lax.broadcasted_iota(jnp.int32, shape, dim)

    lane = iota((1, cols), 1)
    at_z = (z + turn * (lane >> 7) + nz) & (nz - 1)
    at_x = jnp.where((lane >> 4) & 1 == 0, x, xt)
    at_c = jnp.where((lane >> 6) & 1 == 0, c, 1 - c)
    col_ids = (
        y * (XN * nz * CORES * 2 * H)
        + ((at_x * nz + at_z) * CORES + at_c) * (2 * H)
        + ((lane >> 5) & 1) * H
        + (lane & 15)
    )

    def row_ids(k):
        r = iota((G, 1), 0)
        of_x = jnp.where((r >> 4) & 1 == 0, x, xi)
        of_y = (y + turn * k + ny) & (ny - 1)
        return ((of_x * nz + z) * CORES + c) * (ny * 2 * H) + of_y * (2 * H) + ((r >> 5) & 1) * H + (r & 15)

    own_lane = iota((G, 128), 0) == iota((G, 128), 1)

    def to_lanes(column):
        return jnp.sum(jnp.where(own_lane, column, 0.0), axis=0, keepdims=True)

    def to_column(lanes):
        return jnp.sum(jnp.where(own_lane, lanes, 0.0), axis=1, keepdims=True)

    def group8(v, op):
        return op(v.reshape(v.shape[0] // 8, 8, v.shape[1]), axis=0)

    def row_pass(k, carry):
        peak, diag = carry
        here = pl.ds(pl.multiple_of(k * G, G), G)
        tile = L[here]
        row_peak = jnp.max(tile, axis=1, keepdims=True)
        terms = jnp.exp(tile - row_peak)
        Er[here] = terms
        Si[0, pl.ds(k, 1)] = to_lanes(row_peak)
        Si[1, pl.ds(k, 1)] = to_lanes(jnp.sum(terms, axis=1, keepdims=True))
        diag = diag + group8(jnp.where(row_ids(k) == col_ids, tile, 0.0), jnp.sum)
        return jnp.maximum(peak, group8(tile, jnp.max)), diag

    start = (jnp.full((8, cols), -jnp.inf, f32), jnp.zeros((8, cols), f32))
    peak8, diag8 = lax.fori_loop(0, ny, row_pass, start)
    col_peak = jnp.max(peak8, axis=0, keepdims=True)
    lanes_n = cols // 128
    diag_sum = functools.reduce(jnp.add, [diag8[:, i * 128 : (i + 1) * 128] for i in range(lanes_n)])

    def col_pass(k, total):
        here = pl.ds(pl.multiple_of(k * G, G), G)
        terms = jnp.exp(L[here] - col_peak)
        L[here] = terms
        return total + group8(terms, jnp.sum)

    col_total = jnp.sum(lax.fori_loop(0, ny, col_pass, jnp.zeros((8, cols), f32)), axis=0, keepdims=True)

    def fold(v):
        return jnp.concatenate([v[:, k * 128 : (k + 1) * 128] for k in range(nz)], axis=0)

    St[0], St[1] = fold(col_peak), fold(col_total)

    at_xt, at_xi = at(x_=xt), at(x_=xi)
    near = [
        comm.send(St, R1t.at[0], at_xt),
        comm.send(Si, R1i, at_xi),
        comm.send(St, R1t.at[1], other),
        comm.send(St, R1t.at[2], at(x_=xt, c_=1 - c)),
    ]
    lane_n = iota((nz, 128), 1)

    def swap_x(v):
        low = (iota(v.shape, 1) >> 4) & 1 == 0
        return jnp.where(low, pltpu.roll(v, 128 - H, 1), pltpu.roll(v, H, 1))

    def swap_core(v):
        v = pltpu.roll(v, G, 1)
        return jnp.concatenate([v[(nz - k) % nz : (nz - k) % nz + 1] for k in range(nz)], axis=0)

    def shift(v, k, n):
        return jnp.concatenate([v[n - k :], v[: n - k]], axis=0)

    peak_t, total_t = St[0], St[1]
    valid_i = iota((ny, 128), 1) < G
    peak_i, total_i = Si[0], jnp.where(valid_i, Si[1], 1.0)
    for copy in near:
        copy.wait_recv()
    pt, tt = merge([
        (peak_t, total_t),
        (swap_x(R1t[0, 0]), swap_x(R1t[0, 1])),
        (swap_core(R1t[1, 0]), swap_core(R1t[1, 1])),
        (swap_x(swap_core(R1t[2, 0])), swap_x(swap_core(R1t[2, 1]))),
    ])
    pi, ti = merge([(peak_i, total_i), (swap_x(R1i[0]), jnp.where(valid_i, swap_x(R1i[1]), 1.0))])
    R2t[0, 0], R2t[0, 1] = pt, tt
    R2i[0, 0], R2i[0, 1] = pi, ti
    far = [comm.send(R2t.at[0], R2t.at[nz - k], ring_z(k)) for k in range(1, nz)]
    far += [comm.send(R2i.at[0], R2i.at[ny - k], ring_y(k)) for k in range(1, ny)]
    for copy in far:
        copy.wait_recv()
    pt, tt = merge([(pt, tt)] + [(shift(R2t[k, 0], k, nz), shift(R2t[k, 1], k, nz)) for k in range(1, nz)])
    pi, ti = merge([(pi, ti)] + [(shift(R2i[k, 0], k, ny), shift(R2i[k, 1], k, ny)) for k in range(1, ny)])
    Ft[...] = jnp.exp(peak_t - pt) / tt
    Fi[...] = jnp.exp(peak_i - pi) / ti

    def own(v):
        i = iota(v.shape, 1)
        mine = (iota(v.shape, 0) == 0) & (i < G) & ((i >> 4) & 1 == 0)
        return jnp.sum(jnp.where(mine, v, 0.0), axis=0, keepdims=True)

    first = iota((8, 128), 0) == 0
    part = own(pt + jnp.log(tt)) + own(pi + jnp.log(ti))
    L1[x * CORES + c] = jnp.where(first, part, 0.0) - 2.0 * diag_sum
    l1 = [comm.send(L1.at[x * CORES + c], L1.at[x * CORES + c], plane(i)) for i in range(1, XN * CORES)]

    col_factor = jnp.concatenate([Ft[k : k + 1] for k in range(nz)], axis=1)

    def weigh(k, _):
        here = pl.ds(pl.multiple_of(k * G, G), G)
        value = Er[here] * to_column(Fi[pl.ds(k, 1)]) + L[here] * col_factor
        value = value - jnp.where(row_ids(k) == col_ids, 2.0, 0.0)
        Wh[here], Wl[here] = split(value)
        return 0

    lax.fori_loop(0, ny, weigh, 0)

    st = Scatter(comm, TP, tx, tpu_, tpd, tqu, tqd, tqx, nz, ring_z(1), ring_z(nz - 1), at(x_=xt))
    si = Scatter(comm, IP, ix, ipu, ipd, iqu, iqd, iqx, ny, ring_y(1), ring_y(ny - 1), at(x_=xi))
    core = {}
    per = block // 128
    order = sorted(range(blocks), key=lambda b: abs(b * per - nz // 2))
    for b in order:
        span = slice(b * block, (b + 1) * block)
        part = dot3(Wh[:, span], Wl[:, span], Ih[...], Il[...], TN)
        for k in range(b * per, (b + 1) * per):
            TP[k] = part[(k - b * per) * 128 : (k - b * per + 1) * 128]
            to = (nz - k) % nz
            core[to] = comm.send(TP.at[k, G : 2 * G], CR.at[to], other)
    half = rws // 2
    for b in (1, 0):
        part = dot3(Wh[b * half : (b + 1) * half], Wl[b * half : (b + 1) * half], Th[...], Tl[...], NN)
        for k in range(ny // 2):
            IP[b * (ny // 2) + k] = part[k * G : (k + 1) * G]
        for k in range(b * (ny // 2), (b + 1) * (ny // 2)):
            si.send_cross(k)
        if b == 1:
            si.launch("q", ny // 2)
            if ny // 2 + 1 < ny:
                si.launch("q", ny // 2 + 1)
    far_first = lambda n: sorted(range(n), key=lambda k: -min(k, n - k))
    for k in far_first(nz):
        core[k].wait_recv()
        TP[k, 0:G] += CR[k]
        st.send_cross(k)
        if k == nz // 2 or k == nz // 2 + 1:
            st.launch("q", k)
    for copy in l1:
        copy.wait_recv()
    L2[y] = functools.reduce(jnp.add, [L1[i] for i in range(XN * CORES)])
    l2 = [comm.send(L2.at[y], L2.at[y], ring_y(k)) for k in range(1, ny)]
    for n, sc in ((ny, si), (nz, st)):
        for k in (n // 2, n // 2 + 1):
            if k < n:
                sc.add_cross(k)
                sc.launch("p", k)
    for n, sc in ((ny, si), (nz, st)):
        for k in far_first(n):
            if k != n // 2 and k != n // 2 + 1:
                sc.add_cross(k)
    for copy in l2:
        copy.wait_recv()
    L3[z] = functools.reduce(jnp.add, [L2[i] for i in range(ny)])
    l3 = [comm.send(L3.at[z], L3.at[z], ring_z(k)) for k in range(1, nz)]
    for s in range(1, max(ny, nz) // 2 + 1):
        for n, sc in ((ny, si), (nz, st)):
            if s <= n // 2:
                sc.step("q", s)
                sc.step("p", s)
    si.finish_q()
    st.finish_q()
    for copy in l3:
        copy.wait_recv()
    samples = XN * nz * CORES * ny * 2 * H
    loss[0, 0] = jnp.sum(functools.reduce(jnp.add, [L3[i] for i in range(nz)])) / (2.0 * samples)
    si.result(image_grad)
    st.result(text_grad)
    comm.drain()


def local(image, text):
    nz = lax.axis_size("row") // (XN * CORES)
    ny = lax.axis_size("col")
    E = image.shape[1]
    cols, rws = nz * 2 * G, ny * G
    vmem = lambda *shape, dtype=f32: pltpu.VMEM(shape, dtype)

    def ring(n):
        ahead, behind = n // 2, max(n - 1 - n // 2, 1)
        return [
            vmem(n, H, E),
            vmem(ahead, H, E),
            vmem(behind, H, E),
            vmem(ahead, 2 * H, E),
            vmem(behind, 2 * H, E),
            vmem(H, E),
        ]

    scratch = [
        vmem(nz, 2 * G, E),
        vmem(ny, G, E),
        vmem(cols, E, dtype=bf16),
        vmem(cols, E, dtype=bf16),
        vmem(rws, E, dtype=bf16),
        vmem(rws, E, dtype=bf16),
        vmem(rws, cols),
        vmem(rws, cols),
        vmem(rws, cols, dtype=bf16),
        vmem(rws, cols, dtype=bf16),
        vmem(nz, 2 * G, E),
        vmem(nz, G, E),
        vmem(ny, G, E),
        *ring(nz),
        *ring(ny),
        vmem(2, nz, 128),
        vmem(2, ny, 128),
        vmem(3, 2, nz, 128),
        vmem(2, ny, 128),
        vmem(nz, 2, nz, 128),
        vmem(ny, 2, ny, 128),
        vmem(nz, 128),
        vmem(ny, 128),
        vmem(XN * CORES, 8, 128),
        vmem(ny, 8, 128),
        vmem(nz, 8, 128),
        pltpu.SemaphoreType.DMA((160,)),
        pltpu.SemaphoreType.DMA((160,)),
    ]
    block = pl.BlockSpec(memory_space=pltpu.VMEM)
    loss, image_grad, text_grad = pl.pallas_call(
        functools.partial(kernel, nz, ny),
        out_shape=(
            jax.ShapeDtypeStruct((1, 1), f32),
            jax.ShapeDtypeStruct(image.shape, f32),
            jax.ShapeDtypeStruct(text.shape, f32),
        ),
        in_specs=[block, block],
        out_specs=(pl.BlockSpec(memory_space=pltpu.SMEM), block, block),
        scratch_shapes=scratch,
        compiler_params=pltpu.CompilerParams(
            collective_id=0, has_side_effects=True, vmem_limit_bytes=48 * 1024 * 1024
        ),
        name="contrastive",
    )(image, text)
    return loss.reshape(()), image_grad, text_grad


def solution(mesh):
    in_specs = (P(("row", "col"), None), P(("col", "row"), None))
    out_specs = (P(), P(("row", "col"), None), P(("col", "row"), None))
    return jax.shard_map(local, mesh=mesh, in_specs=in_specs, out_specs=out_specs, check_vma=False)
```

time: 610 us -> 98.8 us (0.16)
  the two profiles are of different devices: /device:TPU:1 before, /device:TPU:8 now
where the time goes in v1:
time: 98.8 us; the launch traced here: 98.6 us
  Pallas kernels  93.2 us (94%)
  local copies, waits for them, and re-layouts  3.06 us (3%)
  between operations  2.41 us (2%)
    pallas_call x1, Pallas kernels, local(): pl.pallas_call(functools.partial(kernel, nz, ny), out_shape=(jax.ShapeDty...  93.2 us
    unnamed x6, local copies, waits for them, and re-layouts  3.06 us

profile of v1, /device:TPU:8, one launch (start us, length us, event | category | flops | bytes accessed | tf_op | source)
XLA Modules:
  0.0 98.6 jit_solution(9631447254959887344)
XLA Ops:
  0.6 0.0 copy-start
  0.6 0.9 copy-done
  1.5 0.0 copy-start.1
  1.5 0.9 copy-done.1
  2.4 93.2 %contrastive.1 = (f32[1,1]{1,0:T(1,128)}, f32[32,768]{1,0:T(8,128)S(1)}, f32[32,768]{1,0:T(8,128)S(1)}) custom-call(f32[32,768]{1,0:T(8,128)S(1)} %copy-done, f32[32,768]{1,0:T(8,128)S(1)} %copy-done.1), custom_call_target="tpu_custom_call" | custom-call | tf_op jit(solution)/shard_map/contrastive/pallas_call | solution.py:484
  96.2 0.6 copy.9
  96.9 0.6 copy.10
Async XLA Ops:
  0.6 0.9 copy-start
  1.5 0.9 copy-start.1

commit v2 on v1

v2 whole, which is shorter than its diff:
```python
import functools
import jax
import jax.numpy as jnp
from jax import lax
from jax.experimental import pallas as pl
from jax.experimental.pallas import tpu as pltpu
from jax.sharding import PartitionSpec as P

logit_scale = 20.0
grad_scale = 0.5 * logit_scale
MESH = pl.DeviceIdType.MESH
XN = 4
CORES = 2
H = 16
TREES = ((0, 0, 1, 2, 3), None, (0, 0, 1, 2, 3), (0, 0, 1, 2, 3))
MESSAGES = 76
SMALL = 39
G = 4 * H
f32 = jnp.float32
bf16 = jnp.bfloat16
NT = (((1,), (1,)), ((), ()))
NN = (((1,), (0,)), ((), ()))
TN = (((0,), (0,)), ((), ()))


def dot3(a_hi, a_lo, b_hi, b_lo, dims):
    def dot(a, b):
        return lax.dot_general(a, b, dims, preferred_element_type=f32)

    return dot(a_hi, b_hi) + (dot(a_hi, b_lo) + dot(a_lo, b_hi))


def split(value):
    high = value.astype(bf16)
    return high, (value - high.astype(f32)).astype(bf16)


def merge(parts):
    peak = functools.reduce(jnp.maximum, [p for p, _ in parts])
    total = functools.reduce(jnp.add, [t * jnp.exp(p - peak) for p, t in parts])
    return peak, total


class Comm:
    def __init__(self, send_sem, recv_sem):
        self.send_sem, self.recv_sem, self.next = send_sem, recv_sem, 0

    def send(self, src, dst, device, group):
        copy = pltpu.make_async_remote_copy(
            src_ref=src,
            dst_ref=dst,
            send_sem=self.send_sem.at[group],
            recv_sem=self.recv_sem.at[self.next],
            device_id=device,
            device_id_type=MESH,
        )
        copy.start()
        self.next += 1
        return copy

    def sent(self, group, like, device):
        pltpu.make_async_remote_copy(
            src_ref=like,
            dst_ref=like,
            send_sem=self.send_sem.at[group],
            recv_sem=self.recv_sem.at[0],
            device_id=device,
            device_id_type=MESH,
        ).wait_send()


class Trees:
    def __init__(self, n):
        self.n, self.ahead, self.behind = n, n // 2, n - 1 - n // 2

    def parent(self, lo, d):
        return TREES[lo // H][d]

    def side(self, k):
        return (k, 1, self.ahead) if k <= self.ahead else (self.n - k, -1, self.behind)

    def sides(self, k):
        return [(0, 1, self.ahead), (0, -1, self.behind)] if k == 0 else [self.side(k)]

    def children(self, lo, d, most):
        return [c for c in range(most, d, -1) if self.parent(lo, c) == d]

    def slot(self, d, way):
        return (way * d) % self.n


class Gather(Trees):
    def __init__(self, comm, buf, n, ring, partner, other, group):
        super().__init__(n)
        self.comm, self.buf, self.at, self.partner, self.other, self.group = comm, buf, ring, partner, other, group
        self.cross, self.ring, self.core = {}, {}, {}

    def start(self):
        self.q_cross = self.comm.send(
            self.buf.at[0, 2 * H : 3 * H], self.buf.at[0, 3 * H : G], self.partner, self.group
        )
        self.forward(0, 0)
        self.send_cross(0)
        self.forward(0, 2 * H)

    def start_cross(self):
        self.q_cross.wait_recv()
        self.forward(0, 3 * H)

    def forward(self, k, lo):
        for d, way, most in self.sides(k):
            for c in self.children(lo, d, most):
                to = self.slot(c, way)
                self.ring[to, lo] = self.comm.send(
                    self.buf.at[k, lo : lo + H],
                    self.buf.at[to, lo : lo + H],
                    self.at((-way * (c - d)) % self.n),
                    self.group,
                )

    def send_cross(self, k):
        self.cross[k] = self.comm.send(
            self.buf.at[k, 0:H], self.buf.at[k, H : 2 * H], self.partner, self.group
        )

    def positions(self, s):
        if s > self.ahead:
            return []
        return sorted({s % self.n, (self.n - s) % self.n} if s <= self.behind else {s})

    def step(self, s, lo):
        for k in self.positions(s):
            self.ring[k, lo].wait_recv()
            self.forward(k, lo)
            if lo == 0:
                self.send_cross(k)

    def pass_core(self, k, lo):
        if self.other is not None:
            to = (self.n - k) % self.n
            self.core[to, lo] = self.comm.send(
                self.buf.at[k, lo : lo + 2 * H], self.buf.at[to, G + lo : G + lo + 2 * H], self.other, 1
            )

    def finish_q(self, s):
        for k in self.positions(s):
            self.pass_core(k, 2 * H)

    def finish_p(self, s):
        for k in self.positions(s):
            self.cross[k].wait_recv()
            self.pass_core(k, 0)


class Scatter(Trees):
    def __init__(self, comm, acc, cross_buf, up_buf, down_buf, q_cross, n, ring, partner, group):
        super().__init__(n)
        self.comm, self.acc, self.cross_buf = comm, acc, cross_buf
        self.bufs, self.q_cross_buf = {1: up_buf, -1: down_buf}, q_cross
        self.at, self.partner, self.group = ring, partner, group
        self.cross, self.rings = {}, {}
        self.far = sorted(range(n), key=lambda k: -min(k, n - k))

    def send_cross(self, k):
        self.cross[k] = self.comm.send(
            self.acc.at[k, H : 2 * H], self.cross_buf.at[k], self.partner, self.group
        )

    def leaf(self, k, lo):
        return not any(self.children(lo, d, most) for d, _, most in self.sides(k))

    def launch(self, k, lo):
        d, way, _ = self.side(k)
        dst = self.bufs[way].at[d - 1, lo : lo + H]
        to = self.at((way * (d - self.parent(lo, d))) % self.n)
        copy = self.comm.send(self.acc.at[k, lo : lo + H], dst, to, self.group)
        self.rings[way, d, lo] = (copy, dst)

    def begin(self, ks):
        for k in ks:
            self.send_cross(k)
        for k in ks:
            for lo in (3 * H, 2 * H):
                if self.leaf(k, lo):
                    self.launch(k, lo)

    def step(self, k, lo):
        if lo == 0:
            self.cross[k].wait_recv()
            self.acc[k, 0:H] += self.cross_buf[k]
            if self.leaf(k, lo):
                self.launch(k, lo)
        if self.leaf(k, lo):
            return
        for d, way, most in self.sides(k):
            for c in self.children(lo, d, most):
                copy, dst = self.rings[way, c, lo]
                copy.wait_recv()
                self.acc[k, lo : lo + H] += dst[...]
        if k:
            self.launch(k, lo)
        elif lo == 3 * H:
            self.last = self.comm.send(self.acc.at[0, lo:G], self.q_cross_buf, self.partner, self.group)

    def result(self, out):
        out[0:H] = self.acc[0, 0:H]
        self.last.wait_recv()
        out[H : 2 * H] = self.acc[0, 2 * H : 3 * H] + self.q_cross_buf[...]


def kernel(nz, ny, image, text, loss, image_grad, text_grad,
           T, I, Th, Tl, Ih, Il, L, Er, Wh, Wl, TP, CR, IP,
           tx, tu, td, tq, ix, iu, id_, iq,
           St, Si, R1t, R1i, R2t, R2i, Ft, Fi, L1, L2, L3, send_sem, recv_sem, own_sem):
    row, y = lax.axis_index("row"), lax.axis_index("col")
    x, z, c = row // (CORES * nz), (row // CORES) % nz, row % CORES
    turn = 1 - 2 * c
    xt = x + 1 - 2 * (x % 2)
    xi = XN - 1 - x

    def at(x_=x, y_=y, z_=z, c_=c):
        return (x_ * (CORES * nz) + z_ * CORES + c_, y_)

    def ring_z(k):
        return at(z_=(z + turn * k + nz) % nz)

    def ring_y(k):
        return at(y_=(y + turn * k + ny) % ny)

    def plane(i):
        j = (x * CORES + c + i) % (XN * CORES)
        return at(x_=j // CORES, c_=j % CORES)

    other = at(c_=1 - c)
    cols, rws = nz * 2 * G, ny * G
    comm = Comm(send_sem, recv_sem)

    own_copies = [
        pltpu.make_async_copy(src.at[h * H : (h + 1) * H], dst.at[0, 2 * h * H : (2 * h + 1) * H], own_sem.at[i, h])
        for i, (src, dst) in enumerate(((text, T), (image, I)))
        for h in (1, 0)
    ]
    for copy in own_copies:
        copy.start()
    barrier = pltpu.get_barrier_semaphore()
    peers = [ring_z(k) for k in range(1, nz)] + [ring_y(k) for k in range(1, ny)]
    peers += [plane(i) for i in range(1, XN * CORES)]
    for peer in peers:
        pl.semaphore_signal(barrier, inc=1, device_id=peer, device_id_type=MESH)
    for copy in own_copies:
        copy.wait()
    pl.semaphore_wait(barrier, len(peers))

    gt = Gather(comm, T, nz, ring_z, at(x_=xt), other, 0)
    gi = Gather(comm, I, ny, ring_y, at(x_=xi), None, 2)
    both = (gt, gi)
    for g in both:
        g.start()
    for g in both:
        g.start_cross()
    for s in range(max(nz, ny) // 2 + 1):
        for lo in (0, 2 * H, 3 * H):
            for g in both:
                if s:
                    g.step(s, lo)
        for g in both:
            g.finish_q(s)
            if s:
                g.finish_p(s - 1)

    block = min(256, cols)
    blocks = cols // block
    per = block // 128
    half = ny // 2
    distance = lambda k, n: min(k, n - k)
    near_first = sorted(range(blocks), key=lambda b: max(distance(k, nz) for k in range(b * per, (b + 1) * per)))

    def take_image(h):
        for k in range(h * half, (h + 1) * half):
            Ih[k * G : (k + 1) * G], Il[k * G : (k + 1) * G] = split(I[k])

    def take_text(b):
        for k in range(b * per, (b + 1) * per):
            gt.core[k, 0].wait_recv()
            gt.core[k, 2 * H].wait_recv()
            first = k * 2 * G
            Th[first : first + 2 * G], Tl[first : first + 2 * G] = split(T[k])

    def logits(rows, b):
        span = slice(b * block, (b + 1) * block)
        L[rows, span] = logit_scale * dot3(Ih[rows], Il[rows], Th[span], Tl[span], NT)

    low, high = slice(0, half * G), slice(half * G, rws)
    take_image(0)
    for b in near_first[:-1]:
        take_text(b)
        logits(low, b)
    for g in both:
        g.finish_p(g.ahead)
    take_image(1)
    for b in near_first[:-1]:
        logits(high, b)
    take_text(near_first[-1])
    logits(slice(0, rws), near_first[-1])

    def all_sent():
        comm.sent(0, T.at[0 : nz // 2, 0 : 2 * G - G // nz], other)
        comm.sent(1, T.at[0 : nz // 2], other)
        comm.sent(2, T.at[0 : ny // 2, 0 : 2 * G - G // ny], other)

    all_sent()
    comm.next = MESSAGES

    def iota(shape, dim):
        return lax.broadcasted_iota(jnp.int32, shape, dim)

    lane = iota((1, cols), 1)
    at_z = (z + turn * (lane >> 7) + nz) & (nz - 1)
    at_x = jnp.where((lane >> 4) & 1 == 0, x, xt)
    at_c = jnp.where((lane >> 6) & 1 == 0, c, 1 - c)
    col_ids = (
        y * (XN * nz * CORES * 2 * H)
        + ((at_x * nz + at_z) * CORES + at_c) * (2 * H)
        + ((lane >> 5) & 1) * H
        + (lane & 15)
    )

    def row_ids(k):
        r = iota((G, 1), 0)
        of_x = jnp.where((r >> 4) & 1 == 0, x, xi)
        of_y = (y + turn * k + ny) & (ny - 1)
        return ((of_x * nz + z) * CORES + c) * (ny * 2 * H) + of_y * (2 * H) + ((r >> 5) & 1) * H + (r & 15)

    own_lane = iota((G, 128), 0) == iota((G, 128), 1)

    def to_lanes(column):
        return jnp.sum(jnp.where(own_lane, column, 0.0), axis=0, keepdims=True)

    def to_column(lanes):
        return jnp.sum(jnp.where(own_lane, lanes, 0.0), axis=1, keepdims=True)

    def group8(v, op):
        return op(v.reshape(v.shape[0] // 8, 8, v.shape[1]), axis=0)

    def row_pass(k, carry):
        peak, diag = carry
        here = pl.ds(pl.multiple_of(k * G, G), G)
        tile = L[here]
        row_peak = jnp.max(tile, axis=1, keepdims=True)
        terms = jnp.exp(tile - row_peak)
        Er[here] = terms
        Si[0, pl.ds(k, 1)] = to_lanes(row_peak)
        Si[1, pl.ds(k, 1)] = to_lanes(jnp.sum(terms, axis=1, keepdims=True))
        diag = diag + group8(jnp.where(row_ids(k) == col_ids, tile, 0.0), jnp.sum)
        return jnp.maximum(peak, group8(tile, jnp.max)), diag

    start = (jnp.full((8, cols), -jnp.inf, f32), jnp.zeros((8, cols), f32))
    peak8, diag8 = lax.fori_loop(0, ny, row_pass, start)
    col_peak = jnp.max(peak8, axis=0, keepdims=True)
    lanes_n = cols // 128
    diag_sum = functools.reduce(jnp.add, [diag8[:, i * 128 : (i + 1) * 128] for i in range(lanes_n)])

    def col_pass(k, total):
        here = pl.ds(pl.multiple_of(k * G, G), G)
        terms = jnp.exp(L[here] - col_peak)
        L[here] = terms
        return total + group8(terms, jnp.sum)

    col_total = jnp.sum(lax.fori_loop(0, ny, col_pass, jnp.zeros((8, cols), f32)), axis=0, keepdims=True)

    def fold(v):
        return jnp.concatenate([v[:, k * 128 : (k + 1) * 128] for k in range(nz)], axis=0)

    St[0], St[1] = fold(col_peak), fold(col_total)

    at_xt, at_xi = at(x_=xt), at(x_=xi)
    near = [
        comm.send(St, R1t.at[0], at_xt, 3),
        comm.send(Si, R1i, at_xi, 7),
        comm.send(St, R1t.at[1], other, 3),
        comm.send(St, R1t.at[2], at(x_=xt, c_=1 - c), 3),
    ]
    lane_n = iota((nz, 128), 1)

    def swap_x(v):
        low = (iota(v.shape, 1) >> 4) & 1 == 0
        return jnp.where(low, pltpu.roll(v, 128 - H, 1), pltpu.roll(v, H, 1))

    def swap_core(v):
        v = pltpu.roll(v, G, 1)
        return jnp.concatenate([v[(nz - k) % nz : (nz - k) % nz + 1] for k in range(nz)], axis=0)

    def shift(v, k, n):
        return jnp.concatenate([v[n - k :], v[: n - k]], axis=0)

    peak_t, total_t = St[0], St[1]
    valid_i = iota((ny, 128), 1) < G
    peak_i, total_i = Si[0], jnp.where(valid_i, Si[1], 1.0)
    for copy in near:
        copy.wait_recv()
    pt, tt = merge([
        (peak_t, total_t),
        (swap_x(R1t[0, 0]), swap_x(R1t[0, 1])),
        (swap_core(R1t[1, 0]), swap_core(R1t[1, 1])),
        (swap_x(swap_core(R1t[2, 0])), swap_x(swap_core(R1t[2, 1]))),
    ])
    pi, ti = merge([(peak_i, total_i), (swap_x(R1i[0]), jnp.where(valid_i, swap_x(R1i[1]), 1.0))])
    R2t[0, 0], R2t[0, 1] = pt, tt
    R2i[0, 0], R2i[0, 1] = pi, ti
    far = [comm.send(R2t.at[0], R2t.at[nz - k], ring_z(k), 8) for k in range(1, nz)]
    far += [comm.send(R2i.at[0], R2i.at[ny - k], ring_y(k), 9) for k in range(1, ny)]
    for copy in far:
        copy.wait_recv()
    pt, tt = merge([(pt, tt)] + [(shift(R2t[k, 0], k, nz), shift(R2t[k, 1], k, nz)) for k in range(1, nz)])
    pi, ti = merge([(pi, ti)] + [(shift(R2i[k, 0], k, ny), shift(R2i[k, 1], k, ny)) for k in range(1, ny)])
    Ft[...] = jnp.exp(peak_t - pt) / tt
    Fi[...] = jnp.exp(peak_i - pi) / ti

    def own(v):
        i = iota(v.shape, 1)
        mine = (iota(v.shape, 0) == 0) & (i < G) & ((i >> 4) & 1 == 0)
        return jnp.sum(jnp.where(mine, v, 0.0), axis=0, keepdims=True)

    first = iota((8, 128), 0) == 0
    part = own(pt + jnp.log(tt)) + own(pi + jnp.log(ti))
    L1[x * CORES + c] = jnp.where(first, part, 0.0) - 2.0 * diag_sum
    l1 = [comm.send(L1.at[x * CORES + c], L1.at[x * CORES + c], plane(i), 4) for i in range(1, XN * CORES)]

    col_factor = jnp.concatenate([Ft[k : k + 1] for k in range(nz)], axis=1)

    def weigh(k, _):
        here = pl.ds(pl.multiple_of(k * G, G), G)
        value = Er[here] * to_column(Fi[pl.ds(k, 1)]) + L[here] * col_factor
        value = value - jnp.where(row_ids(k) == col_ids, 2.0, 0.0)
        Wh[here], Wl[here] = split(value)
        return 0

    lax.fori_loop(0, ny, weigh, 0)

    small, comm.next = comm.next, 0
    st = Scatter(comm, TP, tx, tu, td, tq, nz, ring_z, at(x_=xt), 0)
    si = Scatter(comm, IP, ix, iu, id_, iq, ny, ring_y, at(x_=xi), 2)
    core, done, added = {}, [], []

    def gradients(b):
        span = slice(b * block, (b + 1) * block)
        part = dot3(Wh[:, span], Wl[:, span], Ih[...], Il[...], TN)
        here = list(range(b * per, (b + 1) * per))
        for i, k in enumerate(here):
            TP[k] = part[i * 128 : (i + 1) * 128]
            to = (nz - k) % nz
            core[to] = comm.send(TP.at[k, G : 2 * G], CR.at[to], other, 1)
        rows = slice(here[0] * G, (here[-1] + 1) * G)
        part = dot3(Wh[rows], Wl[rows], Th[...], Tl[...], NN)
        for i, k in enumerate(here):
            IP[k] = part[i * G : (i + 1) * G]
        si.begin([k for k in si.far if k in here])
        done.extend(here)
        ready = [k for k in st.far if k in done and (nz - k) % nz in done and k not in added]
        for k in ready:
            core[k].wait_recv()
            TP[k, 0:G] += CR[k]
        added.extend(ready)
        st.begin(ready)

    steps = [(d, lo) for d in range(nz // 2, -1, -1) for lo in (3 * H, 2 * H, 0)]

    def run(some):
        for d, lo in some:
            for sc in (si, st):
                for k in sorted({d, (nz - d) % nz}):
                    if k <= sc.ahead or d <= sc.behind:
                        sc.step(k, lo)

    early = 5 if blocks > 2 else 0
    for b in near_first[:0:-1]:
        gradients(b)
    run(steps[:early])
    gradients(near_first[0])
    sums, comm.next = comm.next, small
    for copy in l1:
        copy.wait_recv()
    L2[y] = functools.reduce(jnp.add, [L1[i] for i in range(XN * CORES)])
    l2 = [comm.send(L2.at[y], L2.at[y], ring_y(k), 5) for k in range(1, ny)]
    small, comm.next = comm.next, sums
    run(steps[early:-3])
    sums, comm.next = comm.next, small
    for copy in l2:
        copy.wait_recv()
    L3[z] = functools.reduce(jnp.add, [L2[i] for i in range(ny)])
    l3 = [comm.send(L3.at[z], L3.at[z], ring_z(k), 6) for k in range(1, nz)]
    small, comm.next = comm.next, sums
    run(steps[-3:])
    for copy in l3:
        copy.wait_recv()
    samples = XN * nz * CORES * ny * 2 * H
    loss[0, 0] = jnp.sum(functools.reduce(jnp.add, [L3[i] for i in range(nz)])) / (2.0 * samples)
    si.result(image_grad)
    st.result(text_grad)
    all_sent()
    comm.sent(3, R1t, other)
    comm.sent(7, R1i, other)
    comm.sent(8, R2t.at[1:], other)
    comm.sent(9, R2i.at[1:], other)
    comm.sent(4, L1.at[1:], other)
    comm.sent(5, L2.at[1:], other)
    comm.sent(6, L3.at[1:], other)


def local(image, text):
    nz = lax.axis_size("row") // (XN * CORES)
    ny = lax.axis_size("col")
    E = image.shape[1]
    cols, rws = nz * 2 * G, ny * G
    vmem = lambda *shape, dtype=f32: pltpu.VMEM(shape, dtype)

    def ring(n):
        ahead, behind = n // 2, max(n - 1 - n // 2, 1)
        return [vmem(n, H, E), vmem(ahead, G, E), vmem(behind, G, E), vmem(H, E)]

    scratch = [
        vmem(nz, 2 * G, E),
        vmem(ny, G, E),
        vmem(cols, E, dtype=bf16),
        vmem(cols, E, dtype=bf16),
        vmem(rws, E, dtype=bf16),
        vmem(rws, E, dtype=bf16),
        vmem(rws, cols),
        vmem(rws, cols),
        vmem(rws, cols, dtype=bf16),
        vmem(rws, cols, dtype=bf16),
        vmem(nz, 2 * G, E),
        vmem(nz, G, E),
        vmem(ny, G, E),
        *ring(nz),
        *ring(ny),
        vmem(2, nz, 128),
        vmem(2, ny, 128),
        vmem(3, 2, nz, 128),
        vmem(2, ny, 128),
        vmem(nz, 2, nz, 128),
        vmem(ny, 2, ny, 128),
        vmem(nz, 128),
        vmem(ny, 128),
        vmem(XN * CORES, 8, 128),
        vmem(ny, 8, 128),
        vmem(nz, 8, 128),
        pltpu.SemaphoreType.DMA((10,)),
        pltpu.SemaphoreType.DMA((MESSAGES + SMALL,)),
        pltpu.SemaphoreType.DMA((2, 2)),
    ]
    block = pl.BlockSpec(memory_space=pltpu.VMEM)
    loss, image_grad, text_grad = pl.pallas_call(
        functools.partial(kernel, nz, ny),
        out_shape=(
            jax.ShapeDtypeStruct((1, 1), f32),
            jax.ShapeDtypeStruct(image.shape, f32),
            jax.ShapeDtypeStruct(text.shape, f32),
        ),
        in_specs=[pl.BlockSpec(memory_space=pltpu.HBM)] * 2,
        out_specs=(pl.BlockSpec(memory_space=pltpu.SMEM), block, block),
        scratch_shapes=scratch,
        compiler_params=pltpu.CompilerParams(
            collective_id=0, has_side_effects=True, vmem_limit_bytes=60 * 1024 * 1024
        ),
        name="contrastive",
    )(image, text)
    return loss.reshape(()), grad_scale * image_grad, grad_scale * text_grad


def solution(mesh):
    in_specs = (P(("row", "col"), None), P(("col", "row"), None))
    out_specs = (P(), P(("row", "col"), None), P(("col", "row"), None))
    return jax.shard_map(local, mesh=mesh, in_specs=in_specs, out_specs=out_specs, check_vma=False)
```

time: 98.8 us -> 80.6 us (0.82)
  the two profiles are of different devices: /device:TPU:8 before, /device:TPU:1 now
where the time goes in v2:
time: 80.6 us; the launch traced here: 80.4 us
  Pallas kernels  76.4 us (95%)
  between operations  2.33 us (3%)
  other arithmetic  1.63 us (2%)
    pallas_call x1, Pallas kernels, local(): pl.pallas_call(functools.partial(kernel, nz, ny), out_shape=(jax.ShapeDty...  76.4 us
    mul x1, other arithmetic, local(): return (loss.reshape(()), grad_scale * image_grad, grad_scale * text_grad)  1.63 us

profile of v2, /device:TPU:1, one launch (start us, length us, event | category | flops | bytes accessed | tf_op | source)
XLA Modules:
  0.0 80.4 jit_solution(14790469068849161640)
XLA Ops:
  0.6 76.4 %contrastive.1 = (f32[1,1]{1,0:T(1,128)}, f32[32,768]{1,0:T(8,128)}, f32[32,768]{1,0:T(8,128)}) custom-call(f32[32,768]{1,0:T(8,128)} %image.1, f32[32,768]{1,0:T(8,128)} %text.1), custom_call_target="tpu_custom_call" | custom-call | tf_op jit(solution)/shard_map/contrastive/pallas_call | solution.py:553
  77.1 1.6 %broadcast_multiply_fusion = (f32[32,768]{1,0:T(8,128)}, f32[32,768]{1,0:T(8,128)}) fusion(f32[32,768]{1,0:T(8,128)} %get-tuple-element.8, f32[32,768]{1,0:T(8,128)} %get-tuple-element.7), kind=kLoop, calls=%fused_computation | loop fusion | flops 49152 | bytes 393216 | tf_op jit(solution)/shard_map/mul | solution.py:568

commit v3 on v2

--- a/solution.py
+++ b/solution.py
@@ -14,7 +14,7 @@
 H = 16
 TREES = ((0, 0, 1, 2, 3), None, (0, 0, 1, 2, 3), (0, 0, 1, 2, 3))
 MESSAGES = 76
-SMALL = 39
+ONE, TEXT, IMAGE, SUM1, SUM2, SUM3 = range(MESSAGES, MESSAGES + 6)
 G = 4 * H
 f32 = jnp.float32
 bf16 = jnp.bfloat16
@@ -45,17 +45,18 @@
     def __init__(self, send_sem, recv_sem):
         self.send_sem, self.recv_sem, self.next = send_sem, recv_sem, 0
 
-    def send(self, src, dst, device, group):
+    def send(self, src, dst, device, group, shared=None):
+        if shared is None:
+            shared, self.next = self.next, self.next + 1
         copy = pltpu.make_async_remote_copy(
             src_ref=src,
             dst_ref=dst,
             send_sem=self.send_sem.at[group],
-            recv_sem=self.recv_sem.at[self.next],
+            recv_sem=self.recv_sem.at[shared],
             device_id=device,
             device_id_type=MESH,
         )
         copy.start()
-        self.next += 1
         return copy
 
     def sent(self, group, like, device):
@@ -67,6 +68,17 @@
             device_id=device,
             device_id_type=MESH,
         ).wait_send()
+
+
+    def received(self, shared, like, device):
+        pltpu.make_async_remote_copy(
+            src_ref=like,
+            dst_ref=like,
+            send_sem=self.send_sem.at[0],
+            recv_sem=self.recv_sem.at[shared],
+            device_id=device,
+            device_id_type=MESH,
+        ).wait_recv()
 
 
 class Trees:
@@ -211,7 +223,7 @@
 def kernel(nz, ny, image, text, loss, image_grad, text_grad,
            T, I, Th, Tl, Ih, Il, L, Er, Wh, Wl, TP, CR, IP,
            tx, tu, td, tq, ix, iu, id_, iq,
-           St, Si, R1t, R1i, R2t, R2i, Ft, Fi, L1, L2, L3, send_sem, recv_sem, own_sem):
+           St, Si, R1t, R2t, R2i, Ft, Fi, L1, L2, L3, send_sem, recv_sem, own_sem):
     row, y = lax.axis_index("row"), lax.axis_index("col")
     x, z, c = row // (CORES * nz), (row // CORES) % nz, row % CORES
     turn = 1 - 2 * c
@@ -221,17 +233,14 @@
     def at(x_=x, y_=y, z_=z, c_=c):
         return (x_ * (CORES * nz) + z_ * CORES + c_, y_)
 
-    def ring_z(k):
-        return at(z_=(z + turn * k + nz) % nz)
-
-    def ring_y(k):
-        return at(y_=(y + turn * k + ny) % ny)
-
-    def plane(i):
-        j = (x * CORES + c + i) % (XN * CORES)
-        return at(x_=j // CORES, c_=j % CORES)
-
-    other = at(c_=1 - c)
+    z_of = [(z + turn * k + nz) % nz for k in range(nz)]
+    y_of = [(y + turn * k + ny) % ny for k in range(ny)]
+    z_ids, y_ids = [at(z_=v) for v in z_of], [at(y_=v) for v in y_of]
+    ring_z, ring_y = z_ids.__getitem__, y_ids.__getitem__
+    places = [(x * CORES + c + i) % (XN * CORES) for i in range(XN * CORES)]
+    plane = [at(x_=j // CORES, c_=j % CORES) for j in places].__getitem__
+    other, at_xt, at_xi = at(c_=1 - c), at(x_=xt), at(x_=xi)
+    across_t, across_i = [at(x_=xt, z_=v) for v in z_of], [at(x_=xi, y_=v) for v in y_of]
     cols, rws = nz * 2 * G, ny * G
     comm = Comm(send_sem, recv_sem)
 
@@ -244,29 +253,35 @@
         copy.start()
     barrier = pltpu.get_barrier_semaphore()
     peers = [ring_z(k) for k in range(1, nz)] + [ring_y(k) for k in range(1, ny)]
-    peers += [plane(i) for i in range(1, XN * CORES)]
+    peers += [plane(i) for i in range(1, XN * CORES)] + across_t[1:] + across_i[1:]
     for peer in peers:
         pl.semaphore_signal(barrier, inc=1, device_id=peer, device_id_type=MESH)
     for copy in own_copies:
         copy.wait()
     pl.semaphore_wait(barrier, len(peers))
 
-    gt = Gather(comm, T, nz, ring_z, at(x_=xt), other, 0)
-    gi = Gather(comm, I, ny, ring_y, at(x_=xi), None, 2)
+    gt = Gather(comm, T, nz, ring_z, at_xt, other, 0)
+    gi = Gather(comm, I, ny, ring_y, at_xi, None, 2)
     both = (gt, gi)
     for g in both:
         g.start()
     for g in both:
         g.start_cross()
-    for s in range(max(nz, ny) // 2 + 1):
-        for lo in (0, 2 * H, 3 * H):
-            for g in both:
-                if s:
-                    g.step(s, lo)
+    def late(s):
+        for g in both:
+            if s:
+                g.step(s, 3 * H)
         for g in both:
             g.finish_q(s)
-            if s:
-                g.finish_p(s - 1)
+        for g in both:
+            g.finish_p(s)
+
+    last = max(nz, ny) // 2
+    for s in range(1, last + 1):
+        for lo in (0, 2 * H):
+            for g in both:
+                g.step(s, lo)
+        late(s - 1)
 
     block = min(256, cols)
     blocks = cols // block
@@ -292,11 +307,13 @@
 
     low, high = slice(0, half * G), slice(half * G, rws)
     take_image(0)
-    for b in near_first[:-1]:
+    for b in near_first[:-2]:
         take_text(b)
         logits(low, b)
-    for g in both:
-        g.finish_p(g.ahead)
+    late(last)
+    for b in near_first[:-1][-1:]:
+        take_text(b)
+        logits(low, b)
     take_image(1)
     for b in near_first[:-1]:
         logits(high, b)
@@ -309,8 +326,6 @@
         comm.sent(2, T.at[0 : ny // 2, 0 : 2 * G - G // ny], other)
 
     all_sent()
-    comm.next = MESSAGES
-
     def iota(shape, dim):
         return lax.broadcasted_iota(jnp.int32, shape, dim)
 
@@ -341,6 +356,11 @@
 
     def group8(v, op):
         return op(v.reshape(v.shape[0] // 8, 8, v.shape[1]), axis=0)
+
+    def share(buf, ids, n, group, shared):
+        for p, ring in enumerate(ids):
+            for k in range(1 - p, n):
+                comm.send(buf.at[0], buf.at[p * n + (n - k) % n], ring[k], group, shared)
 
     def row_pass(k, carry):
         peak, diag = carry
@@ -357,6 +377,9 @@
     start = (jnp.full((8, cols), -jnp.inf, f32), jnp.zeros((8, cols), f32))
     peak8, diag8 = lax.fori_loop(0, ny, row_pass, start)
     col_peak = jnp.max(peak8, axis=0, keepdims=True)
+    valid = iota((ny, 128), 1) < G
+    R2i[0] = jnp.where(valid, Si[0], pltpu.roll(Si[1], G, 1))
+    share(R2i, [y_ids, across_i], ny, 8, IMAGE)
     lanes_n = cols // 128
     diag_sum = functools.reduce(jnp.add, [diag8[:, i * 128 : (i + 1) * 128] for i in range(lanes_n)])
 
@@ -373,14 +396,7 @@
 
     St[0], St[1] = fold(col_peak), fold(col_total)
 
-    at_xt, at_xi = at(x_=xt), at(x_=xi)
-    near = [
-        comm.send(St, R1t.at[0], at_xt, 3),
-        comm.send(Si, R1i, at_xi, 7),
-        comm.send(St, R1t.at[1], other, 3),
-        comm.send(St, R1t.at[2], at(x_=xt, c_=1 - c), 3),
-    ]
-    lane_n = iota((nz, 128), 1)
+    comm.send(St, R1t, other, 3, ONE)
 
     def swap_x(v):
         low = (iota(v.shape, 1) >> 4) & 1 == 0
@@ -393,26 +409,23 @@
     def shift(v, k, n):
         return jnp.concatenate([v[n - k :], v[: n - k]], axis=0)
 
-    peak_t, total_t = St[0], St[1]
-    valid_i = iota((ny, 128), 1) < G
-    peak_i, total_i = Si[0], jnp.where(valid_i, Si[1], 1.0)
-    for copy in near:
-        copy.wait_recv()
-    pt, tt = merge([
-        (peak_t, total_t),
-        (swap_x(R1t[0, 0]), swap_x(R1t[0, 1])),
-        (swap_core(R1t[1, 0]), swap_core(R1t[1, 1])),
-        (swap_x(swap_core(R1t[2, 0])), swap_x(swap_core(R1t[2, 1]))),
+    def ring_of(buf, n):
+        for p in range(2):
+            for k in range(n):
+                v = swap_x(buf[p * n + k]) if p else buf[k]
+                yield shift(v, k, n) if k else v
+
+    peak_t, peak_i = St[0], Si[0]
+    comm.received(ONE, R1t, other)
+    pt, tt = merge([(peak_t, St[1]), (swap_core(R1t[0]), swap_core(R1t[1]))])
+    R2t[0] = pt + jnp.log(tt)
+    share(R2t, [z_ids, across_t], nz, 7, TEXT)
+    comm.received(IMAGE, R2i.at[1:], other)
+    pi, ti = merge([
+        (jnp.where(valid, v, 0.0), jnp.where(valid, pltpu.roll(v, G, 1), 1.0)) for v in ring_of(R2i, ny)
     ])
-    pi, ti = merge([(peak_i, total_i), (swap_x(R1i[0]), jnp.where(valid_i, swap_x(R1i[1]), 1.0))])
-    R2t[0, 0], R2t[0, 1] = pt, tt
-    R2i[0, 0], R2i[0, 1] = pi, ti
-    far = [comm.send(R2t.at[0], R2t.at[nz - k], ring_z(k), 8) for k in range(1, nz)]
-    far += [comm.send(R2i.at[0], R2i.at[ny - k], ring_y(k), 9) for k in range(1, ny)]
-    for copy in far:
-        copy.wait_recv()
-    pt, tt = merge([(pt, tt)] + [(shift(R2t[k, 0], k, nz), shift(R2t[k, 1], k, nz)) for k in range(1, nz)])
-    pi, ti = merge([(pi, ti)] + [(shift(R2i[k, 0], k, ny), shift(R2i[k, 1], k, ny)) for k in range(1, ny)])
+    comm.received(TEXT, R2t.at[1:], other)
+    pt, tt = merge([(v, 1.0) for v in ring_of(R2t, nz)])
     Ft[...] = jnp.exp(peak_t - pt) / tt
     Fi[...] = jnp.exp(peak_i - pi) / ti
 
@@ -424,7 +437,8 @@
     first = iota((8, 128), 0) == 0
     part = own(pt + jnp.log(tt)) + own(pi + jnp.log(ti))
     L1[x * CORES + c] = jnp.where(first, part, 0.0) - 2.0 * diag_sum
-    l1 = [comm.send(L1.at[x * CORES + c], L1.at[x * CORES + c], plane(i), 4) for i in range(1, XN * CORES)]
+    for i in range(1, XN * CORES):
+        comm.send(L1.at[x * CORES + c], L1.at[x * CORES + c], plane(i), 4, SUM1)
 
     col_factor = jnp.concatenate([Ft[k : k + 1] for k in range(nz)], axis=1)
 
@@ -437,9 +451,9 @@
 
     lax.fori_loop(0, ny, weigh, 0)
 
-    small, comm.next = comm.next, 0
-    st = Scatter(comm, TP, tx, tu, td, tq, nz, ring_z, at(x_=xt), 0)
-    si = Scatter(comm, IP, ix, iu, id_, iq, ny, ring_y, at(x_=xi), 2)
+    comm.next = 0
+    st = Scatter(comm, TP, tx, tu, td, tq, nz, ring_z, at_xt, 0)
+    si = Scatter(comm, IP, ix, iu, id_, iq, ny, ring_y, at_xi, 2)
     core, done, added = {}, [], []
 
     def gradients(b):
@@ -475,33 +489,28 @@
     early = 5 if blocks > 2 else 0
     for b in near_first[:0:-1]:
         gradients(b)
+    comm.received(SUM1, L1.at[1:], other)
+    L2[y] = functools.reduce(jnp.add, [L1[i] for i in range(XN * CORES)])
+    for k in range(1, ny):
+        comm.send(L2.at[y], L2.at[y], ring_y(k), 5, SUM2)
     run(steps[:early])
     gradients(near_first[0])
-    sums, comm.next = comm.next, small
-    for copy in l1:
-        copy.wait_recv()
-    L2[y] = functools.reduce(jnp.add, [L1[i] for i in range(XN * CORES)])
-    l2 = [comm.send(L2.at[y], L2.at[y], ring_y(k), 5) for k in range(1, ny)]
-    small, comm.next = comm.next, sums
-    run(steps[early:-3])
-    sums, comm.next = comm.next, small
-    for copy in l2:
-        copy.wait_recv()
+    run(steps[early : early + 1])
+    comm.received(SUM2, L2.at[1:], other)
     L3[z] = functools.reduce(jnp.add, [L2[i] for i in range(ny)])
-    l3 = [comm.send(L3.at[z], L3.at[z], ring_z(k), 6) for k in range(1, nz)]
-    small, comm.next = comm.next, sums
-    run(steps[-3:])
-    for copy in l3:
-        copy.wait_recv()
+    for k in range(1, nz):
+        comm.send(L3.at[z], L3.at[z], ring_z(k), 6, SUM3)
+    run(steps[early + 1 : -3])
+    comm.received(SUM3, L3.at[1:], other)
     samples = XN * nz * CORES * ny * 2 * H
     loss[0, 0] = jnp.sum(functools.reduce(jnp.add, [L3[i] for i in range(nz)])) / (2.0 * samples)
+    run(steps[-3:])
     si.result(image_grad)
     st.result(text_grad)
     all_sent()
     comm.sent(3, R1t, other)
-    comm.sent(7, R1i, other)
-    comm.sent(8, R2t.at[1:], other)
-    comm.sent(9, R2i.at[1:], other)
+    comm.sent(7, R2t.at[1:], other)
+    comm.sent(8, R2i.at[1:], other)
     comm.sent(4, L1.at[1:], other)
     comm.sent(5, L2.at[1:], other)
     comm.sent(6, L3.at[1:], other)
@@ -536,17 +545,16 @@
         *ring(ny),
         vmem(2, nz, 128),
         vmem(2, ny, 128),
-        vmem(3, 2, nz, 128),
-        vmem(2, ny, 128),
-        vmem(nz, 2, nz, 128),
-        vmem(ny, 2, ny, 128),
+        vmem(2, nz, 128),
+        vmem(2 * nz, nz, 128),
+        vmem(2 * ny, ny, 128),
         vmem(nz, 128),
         vmem(ny, 128),
         vmem(XN * CORES, 8, 128),
         vmem(ny, 8, 128),
         vmem(nz, 8, 128),
-        pltpu.SemaphoreType.DMA((10,)),
-        pltpu.SemaphoreType.DMA((MESSAGES + SMALL,)),
+        pltpu.SemaphoreType.DMA((9,)),
+        pltpu.SemaphoreType.DMA((MESSAGES + 6,)),
         pltpu.SemaphoreType.DMA((2, 2)),
     ]
     block = pl.BlockSpec(memory_space=pltpu.VMEM)

time: 80.6 us -> 78.4 us (0.973)
  Pallas kernels: 76.4 us -> 73.5 us
    pallas_call x1, Pallas kernels: 76.4 us -> 73.5 us  [local(): pl.pallas_call(functools.partial(kernel, nz, ny), out_shape=(jax.ShapeDty...]
where the time goes in v3:
time: 78.4 us; the launch traced here: 77.5 us
  Pallas kernels  73.5 us (94%)
  between operations  2.33 us (3%)
  other arithmetic  1.63 us (2%)
    pallas_call x1, Pallas kernels, local(): pl.pallas_call(functools.partial(kernel, nz, ny), out_shape=(jax.ShapeDty...  73.5 us
    mul x1, other arithmetic, local(): return (loss.reshape(()), grad_scale * image_grad, grad_scale * text_grad)  1.63 us

profile of v3, /device:TPU:1, one launch (start us, length us, event | category | flops | bytes accessed | tf_op | source)
XLA Modules:
  0.0 77.5 jit_solution(9135300569773655696)
XLA Ops:
  0.6 73.5 %contrastive.1 = (f32[1,1]{1,0:T(1,128)}, f32[32,768]{1,0:T(8,128)}, f32[32,768]{1,0:T(8,128)}) custom-call(f32[32,768]{1,0:T(8,128)} %image.1, f32[32,768]{1,0:T(8,128)} %text.1), custom_call_target="tpu_custom_call" | custom-call | tf_op jit(solution)/shard_map/contrastive/pallas_call | solution.py:561
  74.2 1.6 %broadcast_multiply_fusion = (f32[32,768]{1,0:T(8,128)}, f32[32,768]{1,0:T(8,128)}) fusion(f32[32,768]{1,0:T(8,128)} %get-tuple-element.8, f32[32,768]{1,0:T(8,128)} %get-tuple-element.7), kind=kLoop, calls=%fused_computation | loop fusion | flops 49152 | bytes 393216 | tf_op jit(solution)/shard_map/mul | solution.py:576

commit v4 on v3

--- a/solution.py
+++ b/solution.py
@@ -454,9 +454,17 @@
     comm.next = 0
     st = Scatter(comm, TP, tx, tu, td, tq, nz, ring_z, at_xt, 0)
     si = Scatter(comm, IP, ix, iu, id_, iq, ny, ring_y, at_xi, 2)
-    core, done, added = {}, [], []
-
-    def gradients(b):
+    core, done, added, pending = {}, [], [], []
+
+    def add_core():
+        for k in pending:
+            core[k].wait_recv()
+            TP[k, 0:G] += CR[k]
+        st.begin(pending)
+        added.extend(pending)
+        pending.clear()
+
+    def gradients(b, image_positions):
         span = slice(b * block, (b + 1) * block)
         part = dot3(Wh[:, span], Wl[:, span], Ih[...], Il[...], TN)
         here = list(range(b * per, (b + 1) * per))
@@ -464,18 +472,15 @@
             TP[k] = part[i * 128 : (i + 1) * 128]
             to = (nz - k) % nz
             core[to] = comm.send(TP.at[k, G : 2 * G], CR.at[to], other, 1)
-        rows = slice(here[0] * G, (here[-1] + 1) * G)
-        part = dot3(Wh[rows], Wl[rows], Th[...], Tl[...], NN)
-        for i, k in enumerate(here):
-            IP[k] = part[i * G : (i + 1) * G]
-        si.begin([k for k in si.far if k in here])
+        add_core()
+        if image_positions:
+            rows = slice(image_positions[0] * G, (image_positions[-1] + 1) * G)
+            part = dot3(Wh[rows], Wl[rows], Th[...], Tl[...], NN)
+            for i, k in enumerate(image_positions):
+                IP[k] = part[i * G : (i + 1) * G]
+            si.begin([k for k in si.far if k in image_positions])
         done.extend(here)
-        ready = [k for k in st.far if k in done and (nz - k) % nz in done and k not in added]
-        for k in ready:
-            core[k].wait_recv()
-            TP[k, 0:G] += CR[k]
-        added.extend(ready)
-        st.begin(ready)
+        pending.extend(k for k in st.far if k in done and (nz - k) % nz in done and k not in added)
 
     steps = [(d, lo) for d in range(nz // 2, -1, -1) for lo in (3 * H, 2 * H, 0)]
 
@@ -487,24 +492,27 @@
                         sc.step(k, lo)
 
     early = 5 if blocks > 2 else 0
-    for b in near_first[:0:-1]:
-        gradients(b)
+    shares = {0: range(half, ny), max(blocks - 3, 1): range(half)} if blocks > 1 else {0: range(ny)}
+    for i, b in enumerate(near_first[:0:-1]):
+        gradients(b, shares.get(i))
+    run(steps[:early])
     comm.received(SUM1, L1.at[1:], other)
     L2[y] = functools.reduce(jnp.add, [L1[i] for i in range(XN * CORES)])
     for k in range(1, ny):
         comm.send(L2.at[y], L2.at[y], ring_y(k), 5, SUM2)
-    run(steps[:early])
-    gradients(near_first[0])
+    gradients(near_first[0], shares.get(blocks - 1))
     run(steps[early : early + 1])
+    add_core()
+    run(steps[early + 1 : early + 3])
     comm.received(SUM2, L2.at[1:], other)
     L3[z] = functools.reduce(jnp.add, [L2[i] for i in range(ny)])
     for k in range(1, nz):
         comm.send(L3.at[z], L3.at[z], ring_z(k), 6, SUM3)
-    run(steps[early + 1 : -3])
+    run(steps[early + 3 : -1])
     comm.received(SUM3, L3.at[1:], other)
     samples = XN * nz * CORES * ny * 2 * H
     loss[0, 0] = jnp.sum(functools.reduce(jnp.add, [L3[i] for i in range(nz)])) / (2.0 * samples)
-    run(steps[-3:])
+    run(steps[-1:])
     si.result(image_grad)
     st.result(text_grad)
     all_sent()

time: 78.4 us -> 78 us (level)
  Pallas kernels: 73.5 us -> 72.6 us
    pallas_call x1, Pallas kernels: 73.5 us -> 72.6 us  [local(): pl.pallas_call(functools.partial(kernel, nz, ny), out_shape=(jax.ShapeDty...]
where the time goes in v4:
time: 78 us; the launch traced here: 76.5 us
  Pallas kernels  72.6 us (93%)
  between operations  2.33 us (3%)
  other arithmetic  1.63 us (2%)
    pallas_call x1, Pallas kernels, local(): pl.pallas_call(functools.partial(kernel, nz, ny), out_shape=(jax.ShapeDty...  72.6 us
    mul x1, other arithmetic, local(): return (loss.reshape(()), grad_scale * image_grad, grad_scale * text_grad)  1.63 us

profile of v4, /device:TPU:1, one launch (start us, length us, event | category | flops | bytes accessed | tf_op | source)
XLA Modules:
  0.0 76.5 jit_solution(16706616854980996683)
XLA Ops:
  0.6 72.6 %contrastive.1 = (f32[1,1]{1,0:T(1,128)}, f32[32,768]{1,0:T(8,128)}, f32[32,768]{1,0:T(8,128)}) custom-call(f32[32,768]{1,0:T(8,128)} %image.1, f32[32,768]{1,0:T(8,128)} %text.1), custom_call_target="tpu_custom_call" | custom-call | tf_op jit(solution)/shard_map/contrastive/pallas_call | solution.py:569
  73.2 1.6 %broadcast_multiply_fusion = (f32[32,768]{1,0:T(8,128)}, f32[32,768]{1,0:T(8,128)}) fusion(f32[32,768]{1,0:T(8,128)} %get-tuple-element.8, f32[32,768]{1,0:T(8,128)} %get-tuple-element.7), kind=kLoop, calls=%fused_computation | loop fusion | flops 49152 | bytes 393216 | tf_op jit(solution)/shard_map/mul | solution.py:584

commit v5 on v4

--- a/solution.py
+++ b/solution.py
@@ -221,7 +221,7 @@
 
 
 def kernel(nz, ny, image, text, loss, image_grad, text_grad,
-           T, I, Th, Tl, Ih, Il, L, Er, Wh, Wl, TP, CR, IP,
+           T, I, Th, Tl, Ih, Il, L, Er, Ec, Wh, Wl, TP, CR, IP,
            tx, tu, td, tq, ix, iu, id_, iq,
            St, Si, R1t, R2t, R2i, Ft, Fi, L1, L2, L3, send_sem, recv_sem, own_sem):
     row, y = lax.axis_index("row"), lax.axis_index("col")
@@ -362,8 +362,7 @@
             for k in range(1 - p, n):
                 comm.send(buf.at[0], buf.at[p * n + (n - k) % n], ring[k], group, shared)
 
-    def row_pass(k, carry):
-        peak, diag = carry
+    def row_pass(k, diag):
         here = pl.ds(pl.multiple_of(k * G, G), G)
         tile = L[here]
         row_peak = jnp.max(tile, axis=1, keepdims=True)
@@ -371,32 +370,34 @@
         Er[here] = terms
         Si[0, pl.ds(k, 1)] = to_lanes(row_peak)
         Si[1, pl.ds(k, 1)] = to_lanes(jnp.sum(terms, axis=1, keepdims=True))
-        diag = diag + group8(jnp.where(row_ids(k) == col_ids, tile, 0.0), jnp.sum)
-        return jnp.maximum(peak, group8(tile, jnp.max)), diag
-
-    start = (jnp.full((8, cols), -jnp.inf, f32), jnp.zeros((8, cols), f32))
-    peak8, diag8 = lax.fori_loop(0, ny, row_pass, start)
+        return diag + group8(jnp.where(row_ids(k) == col_ids, tile, 0.0), jnp.sum)
+
+    def peak_pass(k, peak):
+        return jnp.maximum(peak, group8(L[pl.ds(pl.multiple_of(k * G, G), G)], jnp.max))
+
+    peak8 = lax.fori_loop(0, ny, peak_pass, jnp.full((8, cols), -jnp.inf, f32))
     col_peak = jnp.max(peak8, axis=0, keepdims=True)
+
+    def col_pass(k, total):
+        here = pl.ds(pl.multiple_of(k * G, G), G)
+        terms = jnp.exp(L[here] - col_peak)
+        Ec[here] = terms
+        return total + group8(terms, jnp.sum)
+
+    col_total = jnp.sum(lax.fori_loop(0, ny, col_pass, jnp.zeros((8, cols), f32)), axis=0, keepdims=True)
+
+    def fold(v):
+        return jnp.concatenate([v[:, k * 128 : (k + 1) * 128] for k in range(nz)], axis=0)
+
+    St[0], St[1] = fold(col_peak), fold(col_total)
+    comm.send(St, R1t, other, 3, ONE)
+    diag8 = lax.fori_loop(0, ny, row_pass, jnp.zeros((8, cols), f32))
     valid = iota((ny, 128), 1) < G
     R2i[0] = jnp.where(valid, Si[0], pltpu.roll(Si[1], G, 1))
     share(R2i, [y_ids, across_i], ny, 8, IMAGE)
     lanes_n = cols // 128
     diag_sum = functools.reduce(jnp.add, [diag8[:, i * 128 : (i + 1) * 128] for i in range(lanes_n)])
 
-    def col_pass(k, total):
-        here = pl.ds(pl.multiple_of(k * G, G), G)
-        terms = jnp.exp(L[here] - col_peak)
-        L[here] = terms
-        return total + group8(terms, jnp.sum)
-
-    col_total = jnp.sum(lax.fori_loop(0, ny, col_pass, jnp.zeros((8, cols), f32)), axis=0, keepdims=True)
-
-    def fold(v):
-        return jnp.concatenate([v[:, k * 128 : (k + 1) * 128] for k in range(nz)], axis=0)
-
-    St[0], St[1] = fold(col_peak), fold(col_total)
-
-    comm.send(St, R1t, other, 3, ONE)
 
     def swap_x(v):
         low = (iota(v.shape, 1) >> 4) & 1 == 0
@@ -444,7 +445,7 @@
 
     def weigh(k, _):
         here = pl.ds(pl.multiple_of(k * G, G), G)
-        value = Er[here] * to_column(Fi[pl.ds(k, 1)]) + L[here] * col_factor
+        value = Er[here] * to_column(Fi[pl.ds(k, 1)]) + Ec[here] * col_factor
         value = value - jnp.where(row_ids(k) == col_ids, 2.0, 0.0)
         Wh[here], Wl[here] = split(value)
         return 0
@@ -542,6 +543,7 @@
         vmem(cols, E, dtype=bf16),
         vmem(rws, E, dtype=bf16),
         vmem(rws, E, dtype=bf16),
+        vmem(rws, cols),
         vmem(rws, cols),
         vmem(rws, cols),
         vmem(rws, cols, dtype=bf16),

time: 78 us -> 77.5 us (level)
  no operation moved by 1% of the time
where the time goes in v5:
time: 77.5 us; the launch traced here: 76.4 us
  Pallas kernels  72.4 us (93%)
  between operations  2.33 us (3%)
  other arithmetic  1.63 us (2%)
    pallas_call x1, Pallas kernels, local(): pl.pallas_call(functools.partial(kernel, nz, ny), out_shape=(jax.ShapeDty...  72.4 us
    mul x1, other arithmetic, local(): return (loss.reshape(()), grad_scale * image_grad, grad_scale * text_grad)  1.63 us

profile of v5, /device:TPU:1, one launch (start us, length us, event | category | flops | bytes accessed | tf_op | source)
XLA Modules:
  0.0 76.4 jit_solution(1190346782333276473)
XLA Ops:
  0.6 72.4 %contrastive.1 = (f32[1,1]{1,0:T(1,128)}, f32[32,768]{1,0:T(8,128)}, f32[32,768]{1,0:T(8,128)}) custom-call(f32[32,768]{1,0:T(8,128)} %image.1, f32[32,768]{1,0:T(8,128)} %text.1), custom_call_target="tpu_custom_call" | custom-call | tf_op jit(solution)/shard_map/contrastive/pallas_call | solution.py:571
  73.1 1.6 %broadcast_multiply_fusion = (f32[32,768]{1,0:T(8,128)}, f32[32,768]{1,0:T(8,128)}) fusion(f32[32,768]{1,0:T(8,128)} %get-tuple-element.8, f32[32,768]{1,0:T(8,128)} %get-tuple-element.7), kind=kLoop, calls=%fused_computation | loop fusion | flops 49152 | bytes 393216 | tf_op jit(solution)/shard_map/mul | solution.py:586
